TPU v7x, 32 devices: a whole 2x2x4 slice. The times are simulated.
32 devices in a mesh: groups: 2 (over y), tensor: 4 (over z), dp: 4 (over x, core).
Axes of the slice: x: 2, y: 2, z: 4, core: 2. Of those that a mesh axis runs over, the one named last changes fastest.
Arguments:
- tokens: bfloat16 [1024, 16384], P(('groups', 'dp'), 'tensor'), parts along dimension 0, may hold values from -6 to 6
- out_grad: bfloat16 [1024, 16384], P(('groups', 'dp'), 'tensor'), parts along dimension 0, may hold values from -6 to 6
- gate_weight: bfloat16 [16384, 8192], P('dp', 'tensor'), may hold values from -0.046875 to 0.046875
- up_weight: bfloat16 [16384, 8192], P('dp', 'tensor'), may hold values from -0.046875 to 0.046875
- down_weight: bfloat16 [8192, 16384], P('dp', 'tensor'), may hold values from -0.0625 to 0.0625
- in_up: bfloat16 [16384, 64], P('tensor'), may hold values from -0.046875 to 0.046875
- out_up: bfloat16 [8192, 64], P('tensor'), may hold values from -0.0625 to 0.0625
- in_down: bfloat16 [8192, 64], P('tensor'), may hold values from -0.0625 to 0.0625
- out_down: bfloat16 [16384, 64], P('tensor'), may hold values from -0.046875 to 0.046875
- doc_ids: int32 [1024], P(('groups', 'dp')), parts along dimension 0, may hold values from 0 to 7, as said below
Outputs:
- log_up: float32 [16, 64, 64], P(('groups', 'dp')), parts along dimension 0
- log_down: float32 [16, 64, 64], P(('groups', 'dp')), parts along dimension 0
There are 2 independent parts, one for each index of `groups`. A program takes and returns all parts, laid end to end along the dimension named above; an argument that names none is the same for every part. Nothing has to cross between parts.
Inputs may be any that keep to these rules, and one draw needn't show every extreme that they name: `doc_ids`: the tokens of dp index b form the aligned block b of 128 tokens; its ids never fall and take every value from b * 2 to b * 2 + 1.
All inputs are finite; a program needn't handle non-finite values.
Results may differ from a plain program's by a relative error of at most 0.003.
Values may be sent and summed in bfloat16 or wider, within the bound.
A program may use at most 512 MiB of HBM per device.

v0:
```python
import jax
import jax.numpy as jnp
from jax import lax
from jax.sharding import PartitionSpec as P

DOCS_DP = 2


def document_gram(onehot, left, right):
    return jnp.einsum("td,tr,ts->drs", onehot, left, right, precision=lax.Precision.HIGHEST)


def shards(
    tokens, out_grad, gate_weight, up_weight, down_weight, in_up, out_up, in_down, out_down, doc_ids
):
    gate_full, up_full, down_full = (
        lax.all_gather(gate_weight, "dp", axis=0, tiled=True),
        lax.all_gather(up_weight, "dp", axis=0, tiled=True),
        lax.all_gather(down_weight, "dp", axis=0, tiled=True),
    )
    a_up_part = jnp.dot(tokens, in_up, preferred_element_type=jnp.float32)
    b_down_part = jnp.dot(out_grad, out_down, preferred_element_type=jnp.float32)
    whole = lax.all_gather(tokens, "tensor", axis=1, tiled=True)
    gate = jnp.dot(whole, gate_full, preferred_element_type=jnp.float32)
    up = jnp.dot(whole, up_full, preferred_element_type=jnp.float32)
    activated = jax.nn.silu(gate)
    hidden = (activated * up).astype(jnp.bfloat16)
    hidden_grad = lax.psum_scatter(
        lax.dot_general(
            down_full, out_grad, (((1,), (1,)), ((), ())), preferred_element_type=jnp.float32
        ),
        "tensor",
        scatter_dimension=0,
        tiled=True,
    ).T
    up_grad = (hidden_grad * activated).astype(jnp.bfloat16)
    b_up_part = jnp.dot(up_grad, out_up, preferred_element_type=jnp.float32)
    a_down_part = jnp.dot(hidden, in_down, preferred_element_type=jnp.float32)
    first_doc = lax.axis_index("dp") * DOCS_DP
    local_docs = doc_ids - first_doc
    onehot = (local_docs[:, None] == jnp.arange(DOCS_DP, dtype=jnp.int32)[None, :]).astype(
        jnp.float32
    )
    a_up, b_up, a_down, b_down = lax.psum(
        (a_up_part, b_up_part, a_down_part, b_down_part), "tensor"
    )
    log_up = document_gram(onehot, a_up, b_up)
    log_down = document_gram(onehot, a_down, b_down)
    return (log_up, log_down)


def solution(mesh):
    placed = (
        P(("groups", "dp"), "tensor"),
        P(("groups", "dp"), "tensor"),
        P("dp", "tensor"),
        P("dp", "tensor"),
        P("dp", "tensor"),
        P("tensor", None),
        P("tensor", None),
        P("tensor", None),
        P("tensor", None),
        P(("groups", "dp")),
    )
    return jax.shard_map(
        shards,
        mesh=mesh,
        in_specs=placed,
        out_specs=(P(("groups", "dp"), None, None), P(("groups", "dp"), None, None)),
        check_vma=False,
    )
```

profile of v0, /device:TPU:30, one launch (start us, length us, event | category | flops | bytes accessed | tf_op | source)
XLA Modules:
  0.0 1398.9 jit_solution(8451171449796086275)
XLA Ops:
  7.2 0.0 copy-start
  7.2 0.0 copy-start.1
  7.2 0.0 copy-start.6
  7.2 0.0 copy-start.2
  7.2 0.0 all-gather.5.cloned.1.call-start
  7.3 0.7 all-gather.5.cloned.1.call-update
  7.9 0.0 copy-start.3
  8.0 0.0 all-gather.7.cloned.1.call-start
  8.0 0.7 all-gather.7.cloned.1.call-update
  8.7 0.0 all-gather.9.cloned.1.call-start
  8.8 0.7 all-gather.9.cloned.1.call-update
  9.4 0.0 all-gather.11.cloned.1.call-start
  9.5 0.5 all-gather.11.cloned.1.call-update
  10.0 0.0 copy-start.4
  10.0 0.0 reduce-scatter.2.cloned.1.call-start
  10.1 392.3 %all-gather.5.cloned.1.call-done = bf16[8192,4096]{1,0:T(8,128)(2,1)} async-done(((bf16[2048,4096]{1,0:T(8,128)(2,1)}), bf16[8192,4096]{1,0:T(8,128)(2,1)}) %all-gather.5.cloned.1.call-update) | async-done | bytes 67108880 | tf_op jit(solution)/shard_map/all_gather | solution.py:19
  402.4 0.0 copy-done
  402.4 30.7 %fusion.16 = f32[8192,128]{0,1:T(8,128)} fusion(bf16[8192,4096]{1,0:T(8,128)(2,1)} %all-gather.5.cloned.1.call-done, bf16[128,4096]{1,0:T(8,128)(2,1)S(1)} %copy-done), kind=kOutput, calls=%fused_computation.22 | convolution fusion | flops 8589934592 | bytes 72351744 | tf_op jit(solution)/shard_map/dot_general | solution.py:29
  433.1 0.0 reduce-scatter.2.cloned.1.call-update
  433.1 0.0 all-reduce.3.cloned.1.call-start
  433.1 0.0 copy-done.6
  433.2 0.0 copy-done.1
  433.2 0.0 copy-done.2
  433.2 1.1 fusion.15
  434.3 0.0 copy-done.3
  434.3 1.1 fusion.18
  435.4 0.0 copy-start.5
  435.4 47.8 %all-gather.7.cloned.1.call-done = bf16[128,16384]{1,0:T(8,128)(2,1)} async-done(((bf16[128,4096]{1,0:T(8,128)(2,1)}), bf16[128,16384]{1,0:T(8,128)(2,1)}) %all-gather.7.cloned.1.call-update) | async-done | bytes 4194320 | tf_op jit(solution)/shard_map/all_gather | solution.py:23
  483.2 394.4 %all-gather.9.cloned.1.call-done = bf16[16384,2048]{1,0:T(8,128)(2,1)} async-done(((bf16[4096,2048]{1,0:T(8,128)(2,1)}), bf16[16384,2048]{1,0:T(8,128)(2,1)}) %all-gather.9.cloned.1.call-update) | async-done | bytes 67108880 | tf_op jit(solution)/shard_map/all_gather | solution.py:17
  877.6 36.7 %fusion.17 = f32[128,2048]{1,0:T(8,128)S(1)} fusion(bf16[128,16384]{1,0:T(8,128)(2,1)} %all-gather.7.cloned.1.call-done, bf16[16384,2048]{1,0:T(8,128)(2,1)} %all-gather.9.cloned.1.call-done), kind=kOutput, calls=%fused_computation.23 | convolution fusion | flops 8589934592 | bytes 72351744 | tf_op jit(solution)/shard_map/dot_general | solution.py:24
  914.3 357.4 %all-gather.11.cloned.1.call-done = bf16[16384,2048]{1,0:T(8,128)(2,1)} async-done(((bf16[4096,2048]{1,0:T(8,128)(2,1)}), bf16[16384,2048]{1,0:T(8,128)(2,1)}) %all-gather.11.cloned.1.call-update) | async-done | bytes 67108880 | tf_op jit(solution)/shard_map/all_gather | solution.py:18
  1271.8 0.0 copy-done.4
  1271.8 25.5 %fusion.1 = f32[128,64]{0,1:T(8,128)} fusion(bf16[2048,64]{0,1:T(8,128)(2,1)S(1)} %copy-done.4, bf16[128,16384]{1,0:T(8,128)(2,1)} %all-gather.7.cloned.1.call-done, bf16[16384,2048]{1,0:T(8,128)(2,1)} %all-gather.11.cloned.1.call-done, f32[128,2048]{1,0:T(8,128)S(1)} %fusion.17), kind=kOutput, calls=%fused_computation.2 | convolution fusion | flops 8625061888 | bytes 72646656 | tf_op jit(solution)/shard_map/dot_general | solution.py:38
  1297.3 53.8 %reduce-scatter.2.cloned.1.call-done = f32[2048,128]{0,1:T(8,128)} async-done(((f32[8192,128]{0,1:T(8,128)}), f32[2048,128]{0,1:T(8,128)}) %reduce-scatter.2.cloned.1.call-update) | async-done | bytes 1048592 | tf_op jit(solution)/shard_map/reduce_scatter | solution.py:28
  1351.1 0.0 copy-done.5
  1351.1 2.3 fusion.3
  1353.4 0.0 all-reduce.3.cloned.1.call-update
  1353.5 35.3 %all-reduce.3.cloned.1.call-done = (f32[128,64]{0,1:T(8,128)}, f32[128,64]{0,1:T(8,128)}, f32[128,64]{0,1:T(8,128)}, f32[128,64]{0,1:T(8,128)}) async-done(((f32[128,64]{0,1:T(8,128)}, f32[128,64]{0,1:T(8,128)}, f32[128,64]{0,1:T(8,128)}, f32[128,64]{0,1:T(8,128)}), (f32[128,64]{0,1:T(8,128)}, f32[128,64]{0,1:T(8,128)}, f32[128,64]{0,1:T(8,128)}, f32[128,64]{0,1:T(8,128)})) %all-reduce.3.cloned.1.call-update) | async-done | bytes 131088 | tf_op jit(solution)/shard_map/psum | solution.py:44
  1388.8 1.6 convolution_bitcast_fusion
  1390.4 1.6 convolution_bitcast_fusion.1
  (2 shorter events, 0.0 us)
Async XLA Ops:
  7.2 395.2 %copy-start = (bf16[128,4096]{1,0:T(8,128)(2,1)S(1)}, bf16[128,4096]{1,0:T(8,128)(2,1)}, u32[]{:S(2)}) copy-start(bf16[128,4096]{1,0:T(8,128)(2,1)} %param.11) | copy-start | bytes 3145732
  7.2 426.0 %copy-start.1 = (bf16[128,4096]{1,0:T(8,128)(2,1)S(1)}, bf16[128,4096]{1,0:T(8,128)(2,1)}, u32[]{:S(2)}) copy-start(bf16[128,4096]{1,0:T(8,128)(2,1)} %param.10) | copy-start | bytes 3145732
  7.2 426.0 %copy-start.6 = (s32[128]{0:T(128)S(1)}, s32[128]{0:T(128)}, u32[]{:S(2)}) copy-start(s32[128]{0:T(128)} %param.19) | copy-start | bytes 1540
  7.2 426.0 %copy-start.2 = (bf16[4096,64]{0,1:T(8,128)(2,1)S(1)}, bf16[4096,64]{0,1:T(8,128)(2,1)}, u32[]{:S(2)}) copy-start(bf16[4096,64]{0,1:T(8,128)(2,1)} %param.15) | copy-start | bytes 1572868
  7.2 395.2 %all-gather.5.cloned.1.call-start = ((), (), s32[]{:S(2)}) async-start(), calls=%async_computation.1 | async-start | bytes 83886080 | tf_op jit(solution)/shard_map/all_gather | solution.py:19
  7.9 426.3 %copy-start.3 = (bf16[4096,64]{0,1:T(8,128)(2,1)S(1)}, bf16[4096,64]{0,1:T(8,128)(2,1)}, u32[]{:S(2)}) copy-start(bf16[4096,64]{0,1:T(8,128)(2,1)} %param.18) | copy-start | bytes 1572868
  8.0 475.2 %all-gather.7.cloned.1.call-start = ((), (), s32[]{:S(2)}) async-start(), calls=%async_computation.3 | async-start | bytes 5242880 | tf_op jit(solution)/shard_map/all_gather | solution.py:23
  8.7 868.9 %all-gather.9.cloned.1.call-start = ((), (), s32[]{:S(2)}) async-start(), calls=%async_computation.4 | async-start | bytes 83886080 | tf_op jit(solution)/shard_map/all_gather | solution.py:17
  9.4 1262.4 %all-gather.11.cloned.1.call-start = ((), (), s32[]{:S(2)}) async-start(), calls=%async_computation.5 | async-start | bytes 83886080 | tf_op jit(solution)/shard_map/all_gather | solution.py:18
  10.0 1261.8 %copy-start.4 = (bf16[2048,64]{0,1:T(8,128)(2,1)S(1)}, bf16[2048,64]{0,1:T(8,128)(2,1)}, u32[]{:S(2)}) copy-start(bf16[2048,64]{0,1:T(8,128)(2,1)} %param.17) | copy-start | bytes 786436
  10.0 1341.1 %reduce-scatter.2.cloned.1.call-start = ((), (), s32[]{:S(2)}) async-start(), calls=%async_computation.2 | async-start | bytes 5242880 | tf_op jit(solution)/shard_map/reduce_scatter | solution.py:28
  433.1 955.7 %all-reduce.3.cloned.1.call-start = ((), (), s32[]{:S(2)}) async-start(), calls=%async_computation.6 | async-start | bytes 262144 | tf_op jit(solution)/shard_map/psum | solution.py:44
  435.4 915.7 %copy-start.5 = (bf16[2048,64]{0,1:T(8,128)(2,1)S(1)}, bf16[2048,64]{0,1:T(8,128)(2,1)}, u32[]{:S(2)}) copy-start(bf16[2048,64]{0,1:T(8,128)(2,1)} %param.16) | copy-start | bytes 786436
Sparse Core Ops, SparseCore 0:
  9.6 392.7 all-gather.4
  403.9 79.1 all-gather.6
  484.7 392.8 all-gather.8
  879.0 392.7 all-gather.10
  1273.9 77.1 reduce-scatter.1
  1354.3 34.4 all-reduce.2
where the time goes:
time: 1400 us
  waiting for transfers between devices  1280 us (91%)
  matrix products  101 us (7%)
  between operations  14.2 us (1%)
    all_gather x1, waiting for transfers between devices, shards(): lax.all_gather(gate_weight, 'dp', axis=0, tiled=True)  394 us
    all_gather x1, waiting for transfers between devices, shards(): lax.all_gather(down_weight, 'dp', axis=0, tiled=True)  392 us
    all_gather x1, waiting for transfers between devices, shards(): lax.all_gather(up_weight, 'dp', axis=0, tiled=True)  357 us
    reduce_scatter x1, waiting for transfers between devices, shards(): lax.psum_scatter(lax.dot_general(down_full, out_grad, (((1,), (1,)), ((),...  53.8 us
    all_gather x1, waiting for transfers between devices, shards(): whole = lax.all_gather(tokens, 'tensor', axis=1, tiled=True)  47.8 us
    dot_general x1, matrix products, shards(): gate = jnp.dot(whole, gate_full, preferred_element_type=jnp.float32)  36.7 us
    psum x1, waiting for transfers between devices, shards(): lax.psum((a_up_part, b_up_part, a_down_part, b_down_part), 'tensor')  35.3 us
    dot_general x1, matrix products, shards(): lax.dot_general(down_full, out_grad, (((1,), (1,)), ((), ())), preferred_...  30.7 us
  transfers between devices with their start and end apart: 6, of which 6 were waited for; matrix products, arithmetic and copies ran while one was open for 7% of the time, Pallas kernels for 0%

commit v1 on v0

v1 whole, which is shorter than its diff:
```python
import jax
import jax.numpy as jnp
from jax import lax
from jax.sharding import PartitionSpec as P

DOCS_DP = 2


def document_gram(onehot, left, right):
    return jnp.einsum("td,tr,ts->drs", onehot, left, right, precision=lax.Precision.HIGHEST)


def make_shards(n_tensor, n_dp):
    per = n_tensor // n_dp

    def shards(
        tokens, out_grad, gate_weight, up_weight, down_weight, in_up, out_up, in_down, out_down, doc_ids
    ):
        rows = tokens.shape[0]
        a_up_part = jnp.dot(tokens, in_up, preferred_element_type=jnp.float32)
        b_down_part = jnp.dot(out_grad, out_down, preferred_element_type=jnp.float32)
        grads = lax.all_gather(out_grad, "dp", axis=0, tiled=True)
        hg_part = lax.dot_general(
            grads, down_weight, (((1,), (1,)), ((), ())), preferred_element_type=jnp.float32
        )
        units = hg_part.shape[1] // per
        hg_part = hg_part.reshape(n_dp, rows, per, units).transpose(2, 0, 1, 3)
        hg_part = hg_part.reshape(per * n_dp * rows, units)
        hg = lax.psum_scatter(hg_part, "tensor", scatter_dimension=0, tiled=True)
        hidden_grad = lax.ppermute(
            hg,
            ("tensor", "dp"),
            [
                (t * n_dp + d, (d * per + t // n_dp) * n_dp + t % n_dp)
                for t in range(n_tensor)
                for d in range(n_dp)
            ],
        )
        whole = lax.all_gather(tokens, "tensor", axis=1, tiled=True)
        mine = lax.all_to_all(whole, "dp", split_axis=1, concat_axis=0, tiled=True)
        gate_part = jnp.dot(mine, gate_weight, preferred_element_type=jnp.float32)
        gate = lax.psum_scatter(gate_part, "dp", scatter_dimension=0, tiled=True)
        up_part = jnp.dot(mine, up_weight, preferred_element_type=jnp.float32)
        up = lax.psum_scatter(up_part, "dp", scatter_dimension=0, tiled=True)
        activated = jax.nn.silu(gate)
        hidden = (activated * up).astype(jnp.bfloat16)
        up_grad = (hidden_grad * activated).astype(jnp.bfloat16)
        b_up_part = jnp.dot(up_grad, out_up, preferred_element_type=jnp.float32)
        a_down_part = jnp.dot(hidden, in_down, preferred_element_type=jnp.float32)
        first_doc = lax.axis_index("dp") * DOCS_DP
        local_docs = doc_ids - first_doc
        onehot = (local_docs[:, None] == jnp.arange(DOCS_DP, dtype=jnp.int32)[None, :]).astype(
            jnp.float32
        )
        a_up, b_up, a_down, b_down = lax.psum(
            (a_up_part, b_up_part, a_down_part, b_down_part), "tensor"
        )
        log_up = document_gram(onehot, a_up, b_up)
        log_down = document_gram(onehot, a_down, b_down)
        return (log_up, log_down)

    return shards


def solution(mesh):
    placed = (
        P(("groups", "dp"), "tensor"),
        P(("groups", "dp"), "tensor"),
        P("dp", "tensor"),
        P("dp", "tensor"),
        P("dp", "tensor"),
        P("tensor", None),
        P("tensor", None),
        P("tensor", None),
        P("tensor", None),
        P(("groups", "dp")),
    )
    return jax.shard_map(
        make_shards(mesh.shape["tensor"], mesh.shape["dp"]),
        mesh=mesh,
        in_specs=placed,
        out_specs=(P(("groups", "dp"), None, None), P(("groups", "dp"), None, None)),
        check_vma=False,
    )
```

time: 1400 us -> 371 us (0.27)
  waiting for transfers between devices: 1280 us -> 233 us
  blocking collectives: 0 us -> 52.8 us
  matrix products: 101 us -> 55.2 us
    all_gather x3 -> x1, waiting for transfers between devices: 1140 us -> 33.8 us  [shards(): grads = lax.all_gather(out_grad, 'dp', axis=0, tiled=True)]
    all_to_all x0 -> x1, blocking collectives: none -> 52.8 us  [shards(): mine = lax.all_to_all(whole, 'dp', split_axis=1, concat_axis=0, tiled=True)]
    reduce_scatter x1 -> x3, waiting for transfers between devices: 53.8 us -> 97.7 us  [the longest x1 49.5 us: shards(): up = lax.psum_scatter(up_part, 'dp', scatter_dimension=0, tiled=True)]
    dot_general x1, matrix products: 25.5 us -> 2.6 us  [shards(): a_down_part = jnp.dot(hidden, in_down, preferred_element_type=jnp.float32)]
    dot_general x2 -> x3, matrix products: 67.4 us -> 44.9 us  [the longest x1 15 us: shards(): gate_part = jnp.dot(mine, gate_weight, preferred_element_type=jnp.float32)]
    all_gather x1, waiting for transfers between devices: 47.8 us -> 65.7 us  [shards(): whole = lax.all_gather(tokens, 'tensor', axis=1, tiled=True)]
  transfers between devices with their start and end apart: 6 -> 7, of which waited for: 6 -> 5; matrix products, arithmetic and copies ran while one was open for 7% -> 16% of each run, Pallas kernels for 0% -> 0%
where the time goes in v1:
time: 371 us; the launch traced here: 367 us
  waiting for transfers between devices  233 us (63%)
  matrix products  55.2 us (15%)
  blocking collectives  52.8 us (14%)
  between operations  14.2 us (4%)
  local copies, waits for them, and re-layouts  8.78 us (2%)
    all_gather x1, waiting for transfers between devices, shards(): whole = lax.all_gather(tokens, 'tensor', axis=1, tiled=True)  65.7 us
    all_to_all x1, blocking collectives, shards(): mine = lax.all_to_all(whole, 'dp', split_axis=1, concat_axis=0, tiled=True)  52.8 us
    reduce_scatter x1, waiting for transfers between devices, shards(): up = lax.psum_scatter(up_part, 'dp', scatter_dimension=0, tiled=True)  49.5 us
    reduce_scatter x1, waiting for transfers between devices, shards(): gate = lax.psum_scatter(gate_part, 'dp', scatter_dimension=0, tiled=True)  48.1 us
    psum x1, waiting for transfers between devices, shards(): lax.psum((a_up_part, b_up_part, a_down_part, b_down_part), 'tensor')  34.6 us
    all_gather x1, waiting for transfers between devices, shards(): grads = lax.all_gather(out_grad, 'dp', axis=0, tiled=True)  33.8 us
    dot_general x1, matrix products, shards(): gate_part = jnp.dot(mine, gate_weight, preferred_element_type=jnp.float32)  15 us
    dot_general x1, matrix products, shards(): lax.dot_general(grads, down_weight, (((1,), (1,)), ((), ())), preferred_e...  15 us
  transfers between devices with their start and end apart: 7, of which 5 were waited for; matrix products, arithmetic and copies ran while one was open for 16% of the time, Pallas kernels for 0%

profile of v1, /device:TPU:30, one launch (start us, length us, event | category | flops | bytes accessed | tf_op | source)
XLA Modules:
  0.0 367.0 jit_solution(7361051272641444)
XLA Ops:
  7.2 0.0 copy-start
  7.2 0.0 all-gather.3.cloned.1.call-start
  7.2 0.7 all-gather.3.cloned.1.call-update
  7.9 0.0 all-gather.5.cloned.1.call-start
  8.0 2.3 copy.12
  10.3 0.0 all-gather.5.cloned.1.call-update
  10.3 0.0 reduce-scatter.4.cloned.1.call-start
  10.3 33.8 %all-gather.3.cloned.1.call-done = bf16[512,4096]{1,0:T(8,128)(2,1)} async-done(((bf16[128,4096]{1,0:T(8,128)(2,1)}), bf16[512,4096]{1,0:T(8,128)(2,1)}) %all-gather.3.cloned.1.call-update) | async-done | bytes 4194320 | tf_op jit(solution)/shard_map/all_gather | solution.py:22
  44.1 15.0 %fusion.13 = f32[512,2048]{1,0:T(8,128)} fusion(bf16[512,4096]{1,0:T(8,128)(2,1)} %all-gather.3.cloned.1.call-done, bf16[2048,4096]{1,0:T(8,128)(2,1)} %param.14), kind=kOutput, calls=%fused_computation.20 | convolution fusion | flops 8589934592 | bytes 25165824 | tf_op jit(solution)/shard_map/dot_general | solution.py:23
  59.1 0.0 reduce-scatter.4.cloned.1.call-update
  59.1 0.0 reduce-scatter.6.cloned.1.call-start
  59.2 65.7 %all-gather.5.cloned.1.call-done = bf16[128,16384]{0,1:T(8,128)(2,1)} async-done(((bf16[128,4096]{0,1:T(8,128)(2,1)}), bf16[128,16384]{0,1:T(8,128)(2,1)}) %all-gather.5.cloned.1.call-update) | async-done | bytes 4194320 | tf_op jit(solution)/shard_map/all_gather | solution.py:39
  124.9 52.8 %all_to_all.19 = bf16[128,4,4096]{0,2,1:T(8,128)(2,1)} all-to-all(bf16[128,4,4096]{0,2,1:T(8,128)(2,1)} %bitcast.26), channel_id=1, replica_groups=mesh['groups'=2,'tensor'=4,'dp'=4] {'dp'}, dimensions={1} | all-to-all | bytes 8388608 | tf_op jit(solution)/shard_map/all_to_all | solution.py:40
  177.6 6.4 %copy.13 = bf16[4,128,4096]{2,1,0:T(8,128)(2,1)} copy(bf16[4,128,4096]{1,2,0:T(8,128)(2,1)} %bitcast.25) | data formatting | bytes 8388608 | tf_op jit(solution)/shard_map/all_to_all | solution.py:40
  184.1 15.0 %fusion.14 = f32[512,2048]{1,0:T(8,128)} fusion(bf16[512,4096]{1,0:T(8,128)(2,1)} %bitcast.27, bf16[4096,2048]{1,0:T(8,128)(2,1)} %param.12), kind=kOutput, calls=%fused_computation.21 | convolution fusion | flops 8589934592 | bytes 25165824 | tf_op jit(solution)/shard_map/dot_general | solution.py:41
  199.1 0.0 reduce-scatter.6.cloned.1.call-update
  199.1 0.0 reduce-scatter.8.cloned.1.call-start
  199.2 14.9 %fusion.15 = f32[512,2048]{1,0:T(8,128)} fusion(bf16[512,4096]{1,0:T(8,128)(2,1)} %bitcast.28, bf16[4096,2048]{1,0:T(8,128)(2,1)} %param.13), kind=kOutput, calls=%fused_computation.22 | convolution fusion | flops 8589934592 | bytes 25165824 | tf_op jit(solution)/shard_map/dot_general | solution.py:43
  214.1 0.0 copy-start.7
  214.1 0.0 copy-start.1
  214.1 0.0 copy-start.2
  214.1 0.0 copy-start.3
  214.1 0.0 copy-start.5
  214.1 0.0 reduce-scatter.8.cloned.1.call-update
  214.1 0.0 all-reduce.3.cloned.1.call-start
  214.2 0.0 reduce-scatter.4.cloned.1.call-done
  214.2 3.2 collective-permute-start
  217.5 0.0 copy-done.7
  217.5 0.0 copy-done
  217.5 0.0 copy-done.1
  217.5 1.1 fusion.12
  218.6 0.0 copy-done.2
  218.6 0.0 copy-done.3
  218.6 0.0 copy-start.6
  218.6 1.1 fusion.16
  219.7 48.1 %reduce-scatter.6.cloned.1.call-done = f32[128,2048]{1,0:T(8,128)} async-done(((f32[512,2048]{1,0:T(8,128)}), f32[128,2048]{1,0:T(8,128)}) %reduce-scatter.6.cloned.1.call-update) | async-done | bytes 1048592 | tf_op jit(solution)/shard_map/reduce_scatter | solution.py:42
  267.8 0.0 copy-start.4
  267.8 49.5 %reduce-scatter.8.cloned.1.call-done = f32[128,2048]{1,0:T(8,128)} async-done(((f32[512,2048]{1,0:T(8,128)}), f32[128,2048]{1,0:T(8,128)}) %reduce-scatter.8.cloned.1.call-update) | async-done | bytes 1048592 | tf_op jit(solution)/shard_map/reduce_scatter | solution.py:44
  317.4 0.0 copy-done.5
  317.4 2.6 fusion.1
  320.0 0.0 collective-permute-done
  320.0 0.0 copy-done.6
  320.0 0.0 copy-done.4
  320.0 2.3 fusion
  322.3 0.0 all-reduce.3.cloned.1.call-update
  322.3 34.6 %all-reduce.3.cloned.1.call-done = (f32[128,64]{0,1:T(8,128)}, f32[128,64]{0,1:T(8,128)}, f32[128,64]{0,1:T(8,128)}, f32[128,64]{0,1:T(8,128)}) async-done(((f32[128,64]{0,1:T(8,128)}, f32[128,64]{0,1:T(8,128)}, f32[128,64]{0,1:T(8,128)}, f32[128,64]{0,1:T(8,128)}), (f32[128,64]{0,1:T(8,128)}, f32[128,64]{0,1:T(8,128)}, f32[128,64]{0,1:T(8,128)}, f32[128,64]{0,1:T(8,128)})) %all-reduce.3.cloned.1.call-update) | async-done | bytes 131088 | tf_op jit(solution)/shard_map/psum | solution.py:55
  356.9 1.6 convolution_bitcast_fusion
  358.5 1.6 convolution_bitcast_fusion.1
  (2 shorter events, 0.0 us)
Async XLA Ops:
  7.2 210.3 %copy-start = (bf16[4096,64]{0,1:T(8,128)(2,1)S(1)}, bf16[4096,64]{0,1:T(8,128)(2,1)}, u32[]{:S(2)}) copy-start(bf16[4096,64]{0,1:T(8,128)(2,1)} %param.15) | copy-start | bytes 1572868
  7.2 36.9 %all-gather.3.cloned.1.call-start = ((), (), s32[]{:S(2)}) async-start(), calls=%async_computation.4 | async-start | bytes 5242880 | tf_op jit(solution)/shard_map/all_gather | solution.py:22
  7.9 117.0 %all-gather.5.cloned.1.call-start = ((), (), s32[]{:S(2)}) async-start(), calls=%async_computation.6 | async-start | bytes 5242880 | tf_op jit(solution)/shard_map/all_gather | solution.py:39
  10.3 203.9 %reduce-scatter.4.cloned.1.call-start = ((), (), s32[]{:S(2)}) async-start(), calls=%async_computation.5 | async-start | bytes 5242880 | tf_op jit(solution)/shard_map/reduce_scatter | solution.py:29
  59.1 208.7 %reduce-scatter.6.cloned.1.call-start = ((), (), s32[]{:S(2)}) async-start(), calls=%async_computation.7 | async-start | bytes 5242880 | tf_op jit(solution)/shard_map/reduce_scatter | solution.py:42
  199.1 118.3 %reduce-scatter.8.cloned.1.call-start = ((), (), s32[]{:S(2)}) async-start(), calls=%async_computation.8 | async-start | bytes 5242880 | tf_op jit(solution)/shard_map/reduce_scatter | solution.py:44
  214.1 3.4 copy-start.7
  214.1 3.4 copy-start.1
  214.1 4.5 %copy-start.2 = (bf16[128,4096]{1,0:T(8,128)(2,1)S(1)}, bf16[128,4096]{1,0:T(8,128)(2,1)}, u32[]{:S(2)}) copy-start(bf16[128,4096]{1,0:T(8,128)(2,1)} %param.11) | copy-start | bytes 3145732
  214.1 4.5 %copy-start.3 = (bf16[4096,64]{0,1:T(8,128)(2,1)S(1)}, bf16[4096,64]{0,1:T(8,128)(2,1)}, u32[]{:S(2)}) copy-start(bf16[4096,64]{0,1:T(8,128)(2,1)} %param.18) | copy-start | bytes 1572868
  214.1 103.3 %copy-start.5 = (bf16[2048,64]{0,1:T(8,128)(2,1)S(1)}, bf16[2048,64]{0,1:T(8,128)(2,1)}, u32[]{:S(2)}) copy-start(bf16[2048,64]{0,1:T(8,128)(2,1)} %param.17) | copy-start | bytes 786436
  214.1 142.8 %all-reduce.3.cloned.1.call-start = ((), (), s32[]{:S(2)}) async-start(), calls=%async_computation.9 | async-start | bytes 262144 | tf_op jit(solution)/shard_map/psum | solution.py:55
  214.2 105.8 %collective-permute-start = (f32[128,2048]{1,0:T(8,128)}, f32[128,2048]{1,0:T(8,128)}, u32[]{:S(2)}, u32[]{:S(2)}) collective-permute-start(f32[128,2048]{1,0:T(8,128)} %reduce-scatter.4.cloned.1.call-done), channel_id=1, source_target_pairs={{0,0},{1,4},{2,8},{3,12},{4,1},{5,5},{6,9},{7,13},{8,2},{9,6},{10,... | collective-permute-start | bytes 3145736 | tf_op jit(solution)/shard_map/ppermute | solution.py:30
  218.6 101.4 %copy-start.6 = (bf16[2048,64]{0,1:T(8,128)(2,1)S(1)}, bf16[2048,64]{0,1:T(8,128)(2,1)}, u32[]{:S(2)}) copy-start(bf16[2048,64]{0,1:T(8,128)(2,1)} %param.16) | copy-start | bytes 786436
  267.8 52.2 %copy-start.4 = (f32[128,2048]{1,0:T(8,128)S(1)}, f32[128,2048]{1,0:T(8,128)}, u32[]{:S(2)}) copy-start(f32[128,2048]{1,0:T(8,128)} %reduce-scatter.6.cloned.1.call-done) | copy-start | bytes 3145732
Sparse Core Ops, SparseCore 0:
  9.6 34.4 all-gather.2
  45.6 79.1 all-gather.4
  127.2 77.2 reduce-scatter.3
  207.0 60.7 reduce-scatter.5
  270.2 47.1 reduce-scatter.7
  322.4 34.4 all-reduce.2

commit v2 on v1

v2 whole, which is shorter than its diff:
```python
import functools

import jax
import jax.numpy as jnp
from jax import lax
from jax.experimental import pallas as pl
from jax.experimental.pallas import tpu as pltpu
from jax.sharding import PartitionSpec as P

DOCS_DP = 2
CHUNKS = 2
SLOTS = 4
PAIR_TYPE = jnp.float32
DOWN_SLOTS = 2
MESH = pl.DeviceIdType.MESH


def document_gram(onehot, left, right):
    return jnp.einsum("td,tr,ts->drs", onehot, left, right, precision=lax.Precision.HIGHEST)


def kernel(
    n_t, n_d,
    tok, og, gate_w, up_w, down_w, in_up, out_up, in_down, out_down,
    fac,
    ring, mine, grads, hg_send, hg_recv, part, sib_recv, pair_send, pair_recv, wbuf, dbuf, fbuf,
    w_sem, d_sem, up_s, dn_s, ring_r, feat_s, feat_r, og_s, og_f, og_r, og_l,
    hg_s, hg_r, sib_s, sib_r, pair_s, pair_r, f_s, f_r,
):
    per = n_t // n_d
    rows, feats = tok.shape
    crow = rows // CHUNKS
    units = out_up.shape[0]
    n_j, _, tile = part.shape[1:]
    half = n_d // 2
    n_h, tile_h = down_w.shape[0] // dbuf.shape[1], dbuf.shape[1]
    g, t, d = lax.axis_index("groups"), lax.axis_index("tensor"), lax.axis_index("dp")

    def remote(src, dst, ss, rs, tt, dd):
        return pltpu.make_async_remote_copy(
            src_ref=src, dst_ref=dst, send_sem=ss, recv_sem=rs,
            device_id=(g, tt, dd), device_id_type=MESH,
        )

    def w_copy(which, j, slot):
        ref = gate_w if which == 0 else up_w
        cols = pl.ds(pl.multiple_of(j * tile, tile), tile)
        return pltpu.make_async_copy(ref.at[:, cols], wbuf.at[slot], w_sem.at[slot])

    def d_copy(h, slot):
        r = pl.ds(pl.multiple_of(h * tile_h, tile_h), tile_h)
        return pltpu.make_async_copy(down_w.at[r, :], dbuf.at[slot], d_sem.at[slot])

    for h in range(min(DOWN_SLOTS, n_h)):
        d_copy(h, h).start()
    for i in range(min(SLOTS, 2 * n_j)):
        w_copy(i % 2, i // 2, i).start()
    own_og = pl.ds(pl.multiple_of(d * rows, rows), rows)
    og_local = pltpu.make_async_copy(og, grads.at[own_og, :], og_l.at[0])
    og_local.start()

    barrier = pltpu.get_barrier_semaphore()

    def greet(i, carry):
        @pl.when(i != t * n_d + d)
        def _():
            pl.semaphore_signal(
                barrier, inc=1, device_id=(g, i // n_d, i % n_d), device_id_type=MESH
            )
        return carry

    lax.fori_loop(0, n_t * n_d, greet, 0)
    pl.semaphore_wait(barrier, n_t * n_d - 1)

    def block(s, c):
        return ring.at[s, pl.ds(c * crow, crow), :]

    def own(c):
        return tok.at[pl.ds(c * crow, crow), :]

    def ring_up(src, s, c):
        return remote(src, block(s, c), up_s.at[s, c], ring_r.at[s, c], t + 1, d)

    def ring_dn(src, s, c):
        return remote(src, block(s, c), dn_s.at[s, c], ring_r.at[s, c], t - 1, d)

    def landing(dd, s, c):
        r = pl.ds(pl.multiple_of(dd * rows + c * crow, crow), crow)
        return mine.at[r, pl.ds(pl.multiple_of((s % per) * feats, 128), feats)]

    def feat_remote(src, s, c):
        return remote(
            src, landing(d, s, c), feat_s.at[s, c], feat_r.at[d, s % per, c], t, s // per
        )

    def feat_local(src, s, c):
        return pltpu.make_async_copy(src, landing(d, s, c), feat_r.at[d, s % per, c])

    def hand_over(src, s, c):
        @pl.when(s // per != d)
        def _():
            feat_remote(src, s, c).start()

        @pl.when(s // per == d)
        def _():
            feat_local(src, s, c).start()

    for c in range(CHUNKS):
        @pl.when(t < n_t - 1)
        def _():
            ring_up(own(c), t, c).start()

        @pl.when(t > 0)
        def _():
            ring_dn(own(c), t, c).start()

        hand_over(own(c), t, c)

    sib = d + 1 - 2 * (d % 2)

    def og_rows(dd):
        return grads.at[pl.ds(pl.multiple_of(dd * rows, rows), rows), :]

    og_first = [remote(og, og_rows(d), og_s.at[0], og_r.at[d], t, sib)]
    for m in range(1, n_d // 2):
        peer = (d + 2 * m) % n_d
        og_first.append(remote(og, og_rows(d), og_s.at[m], og_r.at[d], t, peer))
    for copy in og_first:
        copy.start()

    fbuf[t, 0] = jnp.dot(tok[...], in_up[...], preferred_element_type=jnp.float32)
    fbuf[t, 1] = jnp.dot(og[...], out_down[...], preferred_element_type=jnp.float32)

    def fac_copy(late, m):
        to = (t + m) % n_t
        return remote(
            fbuf.at[t, pl.ds(2 * late, 2)], fbuf.at[t, pl.ds(2 * late, 2)],
            f_s.at[late, m], f_r.at[late, t], to, d,
        )

    def fac_wait(late, m):
        s = (t + m) % n_t
        remote(
            fbuf.at[s, pl.ds(2 * late, 2)], fbuf.at[s, pl.ds(2 * late, 2)],
            f_s.at[late, m], f_r.at[late, s], t, d,
        ).wait_recv()

    def step(k):
        for c in range(CHUNKS):
            s = t - k

            @pl.when(s >= 0)
            def _():
                ring_up(block(s, c), s, c).wait_recv()

                @pl.when(t < n_t - 1)
                def _():
                    ring_up(block(s, c), s, c).start()

                hand_over(block(s, c), s, c)

            r = t + k

            @pl.when(r < n_t)
            def _():
                ring_dn(block(r, c), r, c).wait_recv()

                @pl.when(t > 0)
                def _():
                    ring_dn(block(r, c), r, c).start()

                hand_over(block(r, c), r, c)

    def hidden_tile(h, carry):
        slot = h % DOWN_SLOTS
        d_copy(h, slot).wait()
        out = lax.dot_general(
            grads[...], dbuf[slot], (((1,), (1,)), ((), ())), preferred_element_type=jnp.float32
        )
        hg_send[:, pl.ds(pl.multiple_of(h * tile_h, tile_h), tile_h)] = out.astype(jnp.bfloat16)

        @pl.when(h + DOWN_SLOTS < n_h)
        def _():
            d_copy(h + DOWN_SLOTS, slot).start()
        return carry

    def og_arrive():
        forwards = []
        for m in range(1, n_d // 2):
            src = (d + n_d - 2 * m) % n_d
            remote(og, og_rows(src), og_s.at[m], og_r.at[src], t, sib).wait_recv()
            f = remote(og_rows(src), og_rows(src), og_f.at[m], og_r.at[src], t, sib)
            f.start()
            forwards.append(f)
        og_local.wait()
        remote(og, og_rows(sib), og_s.at[0], og_r.at[sib], t, sib).wait_recv()
        for m in range(1, n_d // 2):
            src = (sib + n_d - 2 * m) % n_d
            remote(og, og_rows(src), og_s.at[m], og_r.at[src], t, sib).wait_recv()
        return forwards

    if n_t <= 8:
        forwards = None
        for k in range(1, n_t):
            step(k)
            if k == 1:
                forwards = og_arrive()
            lo, hi = (k - 1) * n_h // (n_t - 1), k * n_h // (n_t - 1)
            lax.fori_loop(lo, hi, hidden_tile, 0)
    else:
        lax.fori_loop(1, n_t, lambda k, carry: (step(k), carry)[1], 0)
        forwards = og_arrive()
        lax.fori_loop(0, n_h, hidden_tile, 0)

    def hg_src(i, b):
        return hg_send.at[pl.ds(b * rows, rows), pl.ds(i * units, units)]

    def hg_remote(i, b):
        return remote(
            hg_src(i, b), hg_recv.at[t], hg_s.at[i, b], hg_r.at[t], d * per + i, b
        )

    def hg_self(i, b):
        return (d * per + i == t) & (d == b)

    for i in range(per):
        for b in range(n_d):
            @pl.when(jnp.logical_not(hg_self(i, b)))
            def _():
                hg_remote(i, b).start()

            @pl.when(hg_self(i, b))
            def _():
                pltpu.make_async_copy(hg_src(i, b), hg_recv.at[t], hg_r.at[t]).start()

    for m in range(1, n_t):
        fac_copy(0, m).start()

    for dd in range(n_d):
        for p in range(per):
            for c in range(CHUNKS):
                s = p
                remote(
                    landing(dd, s, c), landing(dd, s, c), feat_s.at[0, c], feat_r.at[dd, p, c],
                    t, d,
                ).wait_recv()

    def block_rows(dd):
        return pl.ds(pl.multiple_of(dd * rows, rows), rows)

    def sib_copy(which, j, m):
        to = (sib + 2 * m) % n_d
        return remote(
            part.at[which, j, block_rows(to), :], sib_recv.at[which, j, m],
            sib_s.at[which, j, m], sib_r.at[which, j, m], t, sib,
        )

    def pair_copy(which, j, m):
        return remote(
            pair_send.at[which, j, m - 1], pair_recv.at[which, j, m - 1],
            pair_s.at[which, j, m - 1], pair_r.at[which, j, m - 1], t, (d + 2 * m) % n_d,
        )

    def pair_up(which, j):
        for m in range(half):
            sib_copy(which, j, m).wait_recv()
            dd = block_rows((d + 2 * m) % n_d)
            total = part[which, j, dd, :] + sib_recv[which, j, m]
            if m == 0:
                part[which, j, dd, :] = total
            else:
                pair_send[which, j, m - 1] = total.astype(pair_send.dtype)
                pair_copy(which, j, m).start()

    def project(j, carry):
        for which in range(2):
            item = 2 * j + which
            slot = item % SLOTS
            w_copy(which, j, slot).wait()
            part[which, j] = jnp.dot(
                mine[...], wbuf[slot], preferred_element_type=jnp.float32
            )
            for m in range(half):
                sib_copy(which, j, m).start()

            @pl.when(item + SLOTS < 2 * n_j)
            def _():
                w_copy(which, j + SLOTS // 2, slot).start()

        @pl.when(j > 0)
        def _():
            for which in range(2):
                pair_up(which, j - 1)
        return carry

    lax.fori_loop(0, n_j, project, 0)
    for which in range(2):
        pair_up(which, n_j - 1)

    for s in range(n_t):
        remote(hg_src(0, 0), hg_recv.at[s], hg_s.at[0, 0], hg_r.at[s], t, d).wait_recv()
    fbuf[t, 2] = jnp.zeros_like(fbuf[t, 2])
    fbuf[t, 3] = jnp.zeros_like(fbuf[t, 3])

    def finish(j, carry):
        sums = []
        for which in range(2):
            total = part[which, j, block_rows(d), :]
            for m in range(1, half):
                pair_copy(which, j, m).wait_recv()
                total = total + pair_recv[which, j, m - 1].astype(jnp.float32)
            sums.append(total)
        gate, up = sums
        cols = pl.ds(pl.multiple_of(j * tile, tile), tile)
        activated = gate / (1.0 + jnp.exp(-gate))
        hidden = (activated * up).astype(jnp.bfloat16)
        hidden_grad = hg_recv[0, :, cols].astype(jnp.float32)
        for s in range(1, n_t):
            hidden_grad = hidden_grad + hg_recv[s, :, cols].astype(jnp.float32)
        up_grad = hidden_grad * activated
        high = up_grad.astype(jnp.bfloat16)
        low = (up_grad - high.astype(jnp.float32)).astype(jnp.bfloat16)
        weight = out_up[cols, :]
        fbuf[t, 2] += jnp.dot(high, weight, preferred_element_type=jnp.float32) + jnp.dot(
            low, weight, preferred_element_type=jnp.float32
        )
        fbuf[t, 3] += jnp.dot(hidden, in_down[cols, :], preferred_element_type=jnp.float32)
        return carry

    lax.fori_loop(0, n_j, finish, 0)
    for m in range(1, n_t):
        fac_copy(1, m).start()
    for late in range(2):
        for m in range(1, n_t):
            fac_wait(late, m)
    fac[...] = jnp.sum(fbuf[...], axis=0)

    for late in range(2):
        for m in range(1, n_t):
            fac_copy(late, m).wait_send()

    def part_done(j, carry):
        for which in range(2):
            for m in range(half):
                sib_copy(which, j, m).wait_send()
            for m in range(1, half):
                pair_copy(which, j, m).wait_send()
        return carry

    lax.fori_loop(0, n_j, part_done, 0)
    for i in range(per):
        for b in range(n_d):
            @pl.when(jnp.logical_not(hg_self(i, b)))
            def _():
                hg_remote(i, b).wait_send()
    for copy in og_first:
        copy.wait_send()
    for copy in forwards:
        copy.wait_send()

    def ring_done(s, carry):
        for c in range(CHUNKS):
            @pl.when((s <= t) & (t < n_t - 1))
            def _():
                ring_up(block(s, c), s, c).wait_send()

            @pl.when((s >= t) & (t > 0))
            def _():
                ring_dn(block(s, c), s, c).wait_send()

            @pl.when(s // per != d)
            def _():
                feat_remote(block(s, c), s, c).wait_send()
        return carry

    lax.fori_loop(0, n_t, ring_done, 0)


def make_shards(n_t, n_d):
    def shards(
        tokens, out_grad, gate_weight, up_weight, down_weight, in_up, out_up, in_down, out_down, doc_ids
    ):
        rows, feats = tokens.shape
        deep, units = gate_weight.shape
        block_units = down_weight.shape[0]
        rank = in_up.shape[1]
        tile = min(256, units)
        tile_h = min(256, block_units)
        n_j = units // tile
        per, half = n_t // n_d, n_d // 2
        bf16, f32 = jnp.bfloat16, jnp.float32
        vmem = pl.BlockSpec(memory_space=pltpu.VMEM)
        hbm = pl.BlockSpec(memory_space=pl.ANY)
        dma = pltpu.SemaphoreType.DMA
        fac = pl.pallas_call(
            functools.partial(kernel, n_t, n_d),
            out_shape=jax.ShapeDtypeStruct((4, rows, rank), f32),
            in_specs=[vmem, vmem, hbm, hbm, hbm, vmem, vmem, vmem, vmem],
            out_specs=vmem,
            scratch_shapes=[
                pltpu.VMEM((n_t, rows, feats), bf16),
                pltpu.VMEM((n_d * rows, deep), bf16),
                pltpu.VMEM((n_d * rows, feats), bf16),
                pltpu.VMEM((n_d * rows, block_units), bf16),
                pltpu.VMEM((n_t, rows, units), bf16),
                pltpu.VMEM((2, n_j, n_d * rows, tile), f32),
                pltpu.VMEM((2, n_j, half, rows, tile), f32),
                pltpu.VMEM((2, n_j, half - 1, rows, tile), PAIR_TYPE),
                pltpu.VMEM((2, n_j, half - 1, rows, tile), PAIR_TYPE),
                pltpu.VMEM((SLOTS, deep, tile), bf16),
                pltpu.VMEM((DOWN_SLOTS, tile_h, feats), bf16),
                pltpu.VMEM((n_t, 4, rows, rank), f32),
                dma((SLOTS,)), dma((DOWN_SLOTS,)),
                dma((n_t, CHUNKS)), dma((n_t, CHUNKS)), dma((n_t, CHUNKS)),
                dma((n_t, CHUNKS)), dma((n_d, per, CHUNKS)),
                dma((n_d,)), dma((n_d,)), dma((n_d,)), dma((1,)),
                dma((per, n_d)), dma((n_t,)),
                dma((2, n_j, half)), dma((2, n_j, half)),
                dma((2, n_j, half - 1)), dma((2, n_j, half - 1)),
                dma((2, n_t)), dma((2, n_t)),
            ],
            compiler_params=pltpu.CompilerParams(
                collective_id=0, has_side_effects=True, vmem_limit_bytes=58 * 2**20
            ),
        )(tokens, out_grad, gate_weight, up_weight, down_weight, in_up, out_up, in_down, out_down)
        a_up, b_down, b_up, a_down = fac[0], fac[1], fac[2], fac[3]
        local_docs = doc_ids - lax.axis_index("dp") * DOCS_DP
        onehot = (local_docs[:, None] == jnp.arange(DOCS_DP, dtype=jnp.int32)[None, :]).astype(
            jnp.float32
        )
        return document_gram(onehot, a_up, b_up), document_gram(onehot, a_down, b_down)

    return shards


def solution(mesh):
    placed = (
        P(("groups", "dp"), "tensor"),
        P(("groups", "dp"), "tensor"),
        P("dp", "tensor"),
        P("dp", "tensor"),
        P("dp", "tensor"),
        P("tensor", None),
        P("tensor", None),
        P("tensor", None),
        P("tensor", None),
        P(("groups", "dp")),
    )
    return jax.shard_map(
        make_shards(mesh.shape["tensor"], mesh.shape["dp"]),
        mesh=mesh,
        in_specs=placed,
        out_specs=(P(("groups", "dp"), None, None), P(("groups", "dp"), None, None)),
        check_vma=False,
    )
```

time: 371 us -> 224 us (0.60); the launches traced: 367 us -> 224 us
  waiting for transfers between devices: 233 us -> 0 us
  Pallas kernels: 0 us -> 210 us
  blocking collectives: 52.8 us -> 0 us
  matrix products: 55.2 us -> 3.37 us
  between operations: 14.2 us -> 0.67 us
    pallas_call x0 -> x1, Pallas kernels: none -> 210 us  [shards(): pl.pallas_call(functools.partial(kernel, n_t, n_d), out_shape=jax.ShapeDt...]
    all_gather x2 -> x0, waiting for transfers between devices: 99.5 us -> none  [the longest x1 65.7 us: shards(): whole = lax.all_gather(tokens, 'tensor', axis=1, tiled=True)]
    reduce_scatter x3 -> x0, waiting for transfers between devices: 97.7 us -> none  [the longest x1 49.5 us: shards(): up = lax.psum_scatter(up_part, 'dp', scatter_dimension=0, tiled=True)]
    all_to_all x1 -> x0, blocking collectives: 52.8 us -> none  [shards(): mine = lax.all_to_all(whole, 'dp', split_axis=1, concat_axis=0, tiled=True)]
    dot_general x7 -> x0, matrix products: 52 us -> none  [the longest x1 15 us: shards(): gate_part = jnp.dot(mine, gate_weight, preferred_element_type=jnp.float32)]
    psum x1 -> x0, waiting for transfers between devices: 34.6 us -> none  [shards(): lax.psum((a_up_part, b_up_part, a_down_part, b_down_part), 'tensor')]
    all_to_all x1 -> x0, local copies, waits for them, and re-layouts: 6.45 us -> none  [shards(): mine = lax.all_to_all(whole, 'dp', split_axis=1, concat_axis=0, tiled=True)]
    unnamed x17 -> x6, local copies, waits for them, and re-layouts: 2.33 us -> 8.7 us
  transfers between devices with their start and end apart: 7 -> 0, of which waited for: 5 -> 0; matrix products, arithmetic and copies ran while one was open for 16% -> 0% of each run, Pallas kernels for 0% -> 0%
where the time goes in v2:
time: 224 us
  Pallas kernels  210 us (94%)
  local copies, waits for them, and re-layouts  9.71 us (4%)
  matrix products  3.37 us (2%)
    pallas_call x1, Pallas kernels, shards(): pl.pallas_call(functools.partial(kernel, n_t, n_d), out_shape=jax.ShapeDt...  210 us
    unnamed x6, local copies, waits for them, and re-layouts  8.7 us

profile of v2, /device:TPU:30, one launch (start us, length us, event | category | flops | bytes accessed | tf_op | source)
XLA Modules:
  0.0 223.7 jit_solution(6775865392729526640)
XLA Ops:
  0.6 2.4 %copy.12.in_up = bf16[4096,64]{1,0:T(8,128)(2,1)} copy(bf16[4096,64]{0,1:T(8,128)(2,1)} %param.15) | data formatting | bytes 1048576 | tf_op args[5]
  3.0 2.4 %copy.15.out_down = bf16[4096,64]{1,0:T(8,128)(2,1)} copy(bf16[4096,64]{0,1:T(8,128)(2,1)} %param.18) | data formatting | bytes 1048576 | tf_op args[8]
  5.4 1.9 copy.13.out_up
  7.4 2.0 copy.14.in_down
  9.3 0.0 copy-start
  9.3 210.0 %shard_map.113 = f32[4,128,64]{2,1,0:T(8,128)} custom-call(bf16[128,4096]{1,0:T(8,128)(2,1)} %tok.1, bf16[128,4096]{1,0:T(8,128)(2,1)} %og.1, bf16[4096,2048]{1,0:T(8,128)(2,1)} %gate_w.1, bf16[4096,2048]{1,0:T(8,128)(2,1)} %up_w.1, bf16[2048,4096]{1,0:T(8,128)(2,1)} %down_w.1, bf16[4096,64]{1,0:T(8,128)(2,1)} %copy.12.in_up, bf16[2048,64]{1,0:T(8,128)(2,1)} %copy.13.out_up, ...), custom_call_target="tpu_custom_call" | custom-call | tf_op jit(solution)/shard_map/pallas_call | solution.py:395
  219.3 0.9 slice_bitcast_fusion
  220.2 0.1 copy.18
  220.3 0.0 copy-done
  220.3 1.7 convolution_bitcast_fusion
  222.0 0.1 copy.16
  222.0 1.7 convolution_bitcast_fusion.1
  (2 shorter events, 0.0 us)
Async XLA Ops:
  9.3 211.0 %copy-start = (s32[128]{0:T(128)S(1)}, s32[128]{0:T(128)}, u32[]{:S(2)}) copy-start(s32[128]{0:T(128)} %param.19) | copy-start | bytes 1540

commit v3 on v2

--- a/solution.py
+++ b/solution.py
@@ -8,11 +8,12 @@
 from jax.sharding import PartitionSpec as P
 
 DOCS_DP = 2
-CHUNKS = 2
+CHUNKS = 4
 SLOTS = 4
 PAIR_TYPE = jnp.float32
 DOWN_SLOTS = 2
 MESH = pl.DeviceIdType.MESH
+ROWS_BY_ROWS = (((1,), (1,)), ((), ()))
 
 
 def document_gram(onehot, left, right):
@@ -30,7 +31,7 @@
     per = n_t // n_d
     rows, feats = tok.shape
     crow = rows // CHUNKS
-    units = out_up.shape[0]
+    units = out_up.shape[1]
     n_j, _, tile = part.shape[1:]
     half = n_d // 2
     n_h, tile_h = down_w.shape[0] // dbuf.shape[1], dbuf.shape[1]
@@ -128,8 +129,12 @@
     for copy in og_first:
         copy.start()
 
-    fbuf[t, 0] = jnp.dot(tok[...], in_up[...], preferred_element_type=jnp.float32)
-    fbuf[t, 1] = jnp.dot(og[...], out_down[...], preferred_element_type=jnp.float32)
+    fbuf[t, 0] = lax.dot_general(
+        tok[...], in_up[...], ROWS_BY_ROWS, preferred_element_type=jnp.float32
+    )
+    fbuf[t, 1] = lax.dot_general(
+        og[...], out_down[...], ROWS_BY_ROWS, preferred_element_type=jnp.float32
+    )
 
     def fac_copy(late, m):
         to = (t + m) % n_t
@@ -320,11 +325,13 @@
         up_grad = hidden_grad * activated
         high = up_grad.astype(jnp.bfloat16)
         low = (up_grad - high.astype(jnp.float32)).astype(jnp.bfloat16)
-        weight = out_up[cols, :]
-        fbuf[t, 2] += jnp.dot(high, weight, preferred_element_type=jnp.float32) + jnp.dot(
-            low, weight, preferred_element_type=jnp.float32
-        )
-        fbuf[t, 3] += jnp.dot(hidden, in_down[cols, :], preferred_element_type=jnp.float32)
+        weight = out_up[:, cols]
+        fbuf[t, 2] += lax.dot_general(
+            high, weight, ROWS_BY_ROWS, preferred_element_type=jnp.float32
+        ) + lax.dot_general(low, weight, ROWS_BY_ROWS, preferred_element_type=jnp.float32)
+        fbuf[t, 3] += lax.dot_general(
+            hidden, in_down[:, cols], ROWS_BY_ROWS, preferred_element_type=jnp.float32
+        )
         return carry
 
     lax.fori_loop(0, n_j, finish, 0)
@@ -422,7 +429,10 @@
             compiler_params=pltpu.CompilerParams(
                 collective_id=0, has_side_effects=True, vmem_limit_bytes=58 * 2**20
             ),
-        )(tokens, out_grad, gate_weight, up_weight, down_weight, in_up, out_up, in_down, out_down)
+        )(
+            tokens, out_grad, gate_weight, up_weight, down_weight,
+            in_up.T, out_up.T, in_down.T, out_down.T,
+        )
         a_up, b_down, b_up, a_down = fac[0], fac[1], fac[2], fac[3]
         local_docs = doc_ids - lax.axis_index("dp") * DOCS_DP
         onehot = (local_docs[:, None] == jnp.arange(DOCS_DP, dtype=jnp.int32)[None, :]).astype(

time: 224 us -> 210 us (0.938)
  local copies, waits for them, and re-layouts: 9.71 us -> 1.01 us
  Pallas kernels: 210 us -> 204 us
    unnamed x6 -> x0, local copies, waits for them, and re-layouts: 8.7 us -> none
    pallas_call x1, Pallas kernels: 210 us -> 204 us  [shards(): pl.pallas_call(functools.partial(kernel, n_t, n_d), out_shape=jax.ShapeDt...]
where the time goes in v3:
time: 210 us
  Pallas kernels  204 us (97%)
  matrix products  3.39 us (2%)
    pallas_call x1, Pallas kernels, shards(): pl.pallas_call(functools.partial(kernel, n_t, n_d), out_shape=jax.ShapeDt...  204 us

profile of v3, /device:TPU:30, one launch (start us, length us, event | category | flops | bytes accessed | tf_op | source)
XLA Modules:
  0.0 210.0 jit_solution(6370456729667343776)
XLA Ops:
  0.6 0.7 broadcast_subtract_fusion
  1.3 204.3 %shard_map.113 = f32[4,128,64]{2,1,0:T(8,128)} custom-call(bf16[128,4096]{1,0:T(8,128)(2,1)} %tok.1, bf16[128,4096]{1,0:T(8,128)(2,1)} %og.1, bf16[4096,2048]{1,0:T(8,128)(2,1)} %gate_w.1, bf16[4096,2048]{1,0:T(8,128)(2,1)} %up_w.1, bf16[2048,4096]{1,0:T(8,128)(2,1)} %down_w.1, bf16[64,4096]{1,0:T(8,128)(2,1)} %bitcast.22, bf16[64,2048]{1,0:T(8,128)(2,1)} %bitcast.24, ...), custom_call_target="tpu_custom_call" | custom-call | tf_op jit(solution)/shard_map/pallas_call | solution.py:402
  205.6 0.9 slice_bitcast_fusion
  206.5 0.1 copy.14
  206.5 1.7 convolution_bitcast_fusion
  208.2 0.1 copy.12
  208.3 1.7 convolution_bitcast_fusion.1
  (1 shorter events, 0.0 us)
